TPU v7x, 256 devices: a whole 4x4x8 slice. The times are simulated.
256 devices in a mesh: dp: 16 (over y_hi, x, core), tensor: 16 (over z, y_lo).
Axes of the slice: x: 4, y: 4 (y_hi: 2, y_lo: 2; y = y_hi * 2 + y_lo), z: 8, core: 2. Of those that a mesh axis runs over, the one named last changes fastest.
Arguments:
- inputs: bfloat16 [8192, 4096], P(('dp', 'tensor')), may hold values from -6 to 6
- cotangent: bfloat16 [8192, 4096], P(('dp', 'tensor')), may hold values from -6 to 6
- gate_up: bfloat16 [2, 8192, 14336], P(None, 'dp', 'tensor'), may hold values from -6 to 6
- down_weight: bfloat16 [14336, 4096], P('tensor'), may hold values from -0.046875 to 0.046875
- proj_model: bfloat16 [4096, 192], replicated
- proj_hidden: bfloat16 [14336, 192], P('tensor')
- lengths: int32 [16], P('dp'), may hold values from 128 to 512
- queries: bfloat16 [256, 12288], P('dp'), may hold values from -6 to 6
Outputs:
- scores: float32 [16, 256], P('dp')
All inputs are finite; a program needn't handle non-finite values.
Results may differ from a plain program's by a relative error of at most 0.0043.
Values may be sent and summed in bfloat16 or wider, within the bound.
A program may use at most 64 MiB of HBM per device.

v0:
```python
import jax
import jax.numpy as jnp
from jax import lax
from jax.sharding import PartitionSpec as P

RANK = 64
LEN = 512


def local_terms(grad_hidden, gate_pre, up_value):
    gate_pre = gate_pre.astype(jnp.float32)
    up_value = up_value.astype(jnp.float32)
    sigma = jax.nn.sigmoid(gate_pre)
    silu_gate = gate_pre * sigma
    hidden = (silu_gate * up_value).astype(jnp.bfloat16)
    grad_up = (grad_hidden * silu_gate).astype(jnp.bfloat16)
    grad_gate = (grad_hidden * up_value * sigma * (1.0 + gate_pre * (1.0 - sigma))).astype(
        jnp.bfloat16
    )
    return (grad_gate, grad_up, hidden)


def project_hidden(parts, proj_hidden):
    columns = []
    for index in range(3):
        block = proj_hidden[:, index * RANK : (index + 1) * RANK]
        columns.append(jnp.dot(parts[index], block, preferred_element_type=jnp.float32))
    return jnp.concatenate(columns, axis=1)


def sketch(weights, model_side, hidden_side):
    inward = (model_side[:, :RANK], model_side[:, RANK : 2 * RANK], hidden_side[:, 2 * RANK :])
    outward = (hidden_side[:, :RANK], hidden_side[:, RANK : 2 * RANK], model_side[:, 2 * RANK :])
    blocks = []
    for source, target in zip(inward, outward):
        scaled = weights[:, :, None] * source[:, None, :]
        blocks.append(jnp.einsum("tei,tj->eij", scaled, target, precision=lax.Precision.HIGHEST))
    stacked = jnp.stack(blocks, axis=1)
    return stacked.reshape(stacked.shape[0], 3 * RANK * RANK)


def live_weights(count, lengths):
    position = jnp.arange(count, dtype=jnp.int32)
    example = position // LEN
    inside = position % LEN
    owners = (example[:, None] == jnp.arange(lengths.shape[0], dtype=jnp.int32)[None, :]).astype(
        jnp.int32
    )
    limit = jnp.sum(owners * lengths[None, :], axis=1)
    live = (inside < limit).astype(jnp.float32)
    return owners.astype(jnp.float32) * live[:, None]


def contract_rows(left, right):
    return lax.dot_general(
        left, right, (((1,), (1,)), ((), ())), preferred_element_type=jnp.float32
    )


def per_device(inputs, cotangent, gate_up, down_weight, proj_model, proj_hidden, lengths, queries):
    row_count = inputs.shape[0]
    all_rows = row_count * lax.axis_size("tensor")
    grad_hidden = contract_rows(
        lax.all_gather(cotangent, "tensor", axis=0, tiled=True), down_weight
    )
    parts = local_terms(grad_hidden, gate_up[0], gate_up[1])
    first_cols = jnp.dot(inputs, proj_model[:, : 2 * RANK], preferred_element_type=jnp.float32)
    second_cols = jnp.dot(cotangent, proj_model[:, 2 * RANK :], preferred_element_type=jnp.float32)
    model_side = jnp.concatenate([first_cols, second_cols], axis=1)
    pieces = tuple((member for member in parts))
    hidden_side = lax.psum(project_hidden(pieces, proj_hidden), "tensor")
    model_all = lax.all_gather(model_side, "tensor", axis=0, tiled=True)
    sketches = sketch(live_weights(all_rows, lengths), model_all, hidden_side)
    norms = jnp.sqrt(jnp.sum(sketches * sketches, axis=1) + 1e-06)
    unit = (sketches / norms[:, None]).astype(jnp.bfloat16)
    return contract_rows(unit, lax.all_gather(queries, "dp", axis=0, tiled=True))


def solution(mesh):
    return jax.shard_map(
        per_device,
        mesh=mesh,
        in_specs=(
            P(("dp", "tensor"), None),
            P(("dp", "tensor"), None),
            P(None, "dp", "tensor"),
            P("tensor", None),
            P(),
            P("tensor", None),
            P("dp"),
            P("dp", None),
        ),
        out_specs=P("dp", None),
        check_vma=False,
    )
```

profile of v0, /device:TPU:2, one launch (start us, length us, event | category | flops | bytes accessed | tf_op | source)
XLA Modules:
  0.0 300.1 jit_solution(11072067471027538610)
XLA Ops:
  7.4 0.0 copy-start
  7.4 0.0 all-gather.3.cloned.1.call-start
  7.4 0.7 all-gather.3.cloned.1.call-update
  8.1 0.0 all-reduce.2.cloned.1.call-start
  8.1 2.1 fusion.11
  10.3 0.0 copy-start.3
  10.3 0.0 copy-start.4
  10.3 101.5 %all-gather.3.cloned.1.call-done = bf16[512,4096]{1,0:T(8,128)(2,1)} async-done(((bf16[32,4096]{1,0:T(8,128)(2,1)}), bf16[512,4096]{1,0:T(8,128)(2,1)}) %all-gather.3.cloned.1.call-update) | async-done | bytes 4194320 | tf_op jit(solution)/shard_map/all_gather | solution.py:64
  111.8 9.9 %fusion.40 = f32[512,896]{1,0:T(8,128)S(1)} fusion(bf16[512,4096]{1,0:T(8,128)(2,1)} %all-gather.3.cloned.1.call-done, bf16[896,4096]{1,0:T(8,128)(2,1)} %param.11), kind=kOutput, calls=%fused_computation.61 | convolution fusion | flops 3758096384 | bytes 13369344 | tf_op jit(solution)/shard_map/dot_general | solution.py:55
  121.7 0.0 copy-done.3
  121.7 0.0 copy-done.4
  121.7 0.6 fusion.10
  122.3 0.9 fusion.14
  123.2 0.0 copy-start.1
  123.2 0.0 copy-start.2
  123.2 1.0 pad_maximum_fusion
  124.2 0.0 all-reduce.2.cloned.1.call-update
  124.2 0.0 all-gather.5.cloned.1.call-start
  124.3 0.5 all-gather.5.cloned.1.call-update
  125.5 0.0 copy-done.1
  125.5 0.3 fusion.19
  125.8 0.0 copy-done
  125.8 0.4 fusion.8
  126.2 35.9 %all_gather.9 = f32[512,192]{1,0:T(8,128)S(1)} all-gather(f32[32,192]{1,0:T(8,128)S(1)} %pad_maximum_fusion.2), channel_id=1, replica_groups=mesh['dp'=16,'tensor'=16] {'tensor'}, dimensions={0}, use_global_device_ids=true | all-gather | bytes 417792 | tf_op jit(solution)/shard_map/all_gather | solution.py:72
  162.1 118.8 %all-reduce.2.cloned.1.call-done = f32[512,192]{1,0:T(8,128)} async-done(((f32[512,192]{1,0:T(8,128)}), f32[512,192]{1,0:T(8,128)}) %all-reduce.2.cloned.1.call-update) | async-done | bytes 393232 | tf_op jit(solution)/shard_map/psum | solution.py:71
  281.0 1.6 convolution_bitcast_fusion.2
  282.6 1.8 convolution_bitcast_fusion.1
  284.5 1.6 convolution_bitcast_fusion
  286.1 0.6 multiply_reduce_fusion
  287.4 0.1 reshape.121
  287.5 0.0 all-gather.5.cloned.1.call-done
  287.6 5.1 %fusion.41 = f32[1,256]{1,0:T(1,128)} fusion(bf16[12288,1]{0,1:T(2,128)(2,1)S(1)} %reshape.121, bf16[256,12288]{1,0:T(8,128)(2,1)} %all-gather.5.cloned.1.call-done), kind=kOutput, calls=%fused_computation.62 | convolution fusion | flops 6291456 | bytes 6317056 | tf_op jit(solution)/shard_map/dot_general | solution.py:55
  (4 shorter events, 0.0 us)
Async XLA Ops:
  7.4 118.4 %copy-start = (bf16[32,4096]{1,0:T(8,128)(2,1)S(1)}, bf16[32,4096]{1,0:T(8,128)(2,1)}, u32[]{:S(2)}) copy-start(bf16[32,4096]{1,0:T(8,128)(2,1)} %param.8) | copy-start | bytes 786436
  7.4 104.4 %all-gather.3.cloned.1.call-start = ((), (), s32[]{:S(2)}) async-start(), calls=%async_computation | async-start | bytes 4456448 | tf_op jit(solution)/shard_map/all_gather | solution.py:64
  8.1 272.9 %all-reduce.2.cloned.1.call-start = ((), (), s32[]{:S(2)}) async-start(), calls=%async_computation.1 | async-start | bytes 1048576 | tf_op jit(solution)/shard_map/psum | solution.py:71
  10.3 111.4 %copy-start.3 = (bf16[2,512,896]{2,1,0:T(8,128)(2,1)S(1)}, bf16[2,512,896]{2,1,0:T(8,128)(2,1)}, u32[]{:S(2)}) copy-start(bf16[2,512,896]{2,1,0:T(8,128)(2,1)} %param.10) | copy-start | bytes 5505028
  10.3 111.4 %copy-start.4 = (bf16[896,192]{0,1:T(8,128)(2,1)S(1)}, bf16[896,192]{0,1:T(8,128)(2,1)}, u32[]{:S(2)}) copy-start(bf16[896,192]{0,1:T(8,128)(2,1)} %param.13) | copy-start | bytes 1032196
  123.2 2.3 copy-start.1
  123.2 2.3 copy-start.2
  124.2 163.3 %all-gather.5.cloned.1.call-start = ((), (), s32[]{:S(2)}) async-start(), calls=%async_computation.2 | async-start | bytes 6684672 | tf_op jit(solution)/shard_map/all_gather | solution.py:76
Sparse Core Ops, SparseCore 0:
  10.0 101.7 all-gather.2
  124.4 156.5 all-reduce.1
Sparse Core Ops, SparseCore 1:
  127.8 71.6 all-gather.4
where the time goes:
time: 300 us
  waiting for transfers between devices  222 us (74%)
  blocking collectives  35.9 us (12%)
  matrix products  24.4 us (8%)
  between operations  16.3 us (5%)
    psum x1, waiting for transfers between devices, per_device(): hidden_side = lax.psum(project_hidden(pieces, proj_hidden), 'tensor')  119 us
    all_gather x1, waiting for transfers between devices, per_device(): lax.all_gather(cotangent, 'tensor', axis=0, tiled=True)  101 us
    all_gather x1, blocking collectives, per_device(): model_all = lax.all_gather(model_side, 'tensor', axis=0, tiled=True)  35.9 us
    dot_general x2, matrix products, contract_rows(): lax.dot_general(left, right, (((1,), (1,)), ((), ())), preferred_element_...  15 us
  transfers between devices with their start and end apart: 3, of which 2 were waited for; matrix products, arithmetic and copies ran while one was open for 3% of the time, Pallas kernels for 0%

commit v1 on v0

v1 whole, which is shorter than its diff:
```python
import jax
import jax.numpy as jnp
from jax import lax
from jax.experimental import pallas as pl
from jax.experimental.pallas import tpu as pltpu
from jax.sharding import PartitionSpec as P

MESH = pl.DeviceIdType.MESH
RANK = 64
N = 16
STEPS = 5
PIECES = 2
D = 4096
FF = 896
ROWS = 32
WIDE = D + 2 * RANK
SLICE = 768
CUTS = tuple((D // PIECES * j, D // PIECES * (j + 1)) for j in range(PIECES))
NT = (((1,), (1,)), ((), ()))
TN = (((0,), (0,)), ((), ()))

DOWN, UP, ACROSS = 0, 1, 2


def span(piece):
    low, high = CUTS[piece]
    return pl.ds(low, (WIDE if piece == PIECES - 1 else high) - low)


def slot_of(step, link):
    return 1 + 3 * (step - 1) + link


def dot(a, b, dims):
    return lax.dot_general(a, b, dims, preferred_element_type=jnp.float32)


def kernel(
    lengths,
    inputs,
    cotangent,
    gate_up,
    down_weight,
    proj_model,
    proj_hidden,
    queries,
    out,
    block,
    weight,
    gates,
    factor_up,
    factor_gate,
    x_rows,
    pm,
    ph,
    hidden_proj,
    grad,
    model_cot,
    total,
    turned,
    parts,
    parts_in,
    query_in,
    tile,
    tiles_in,
    load_sem,
    gate_sem,
    send_sem,
    recv_sem,
    query_send,
    query_recv,
    parts_send,
    parts_recv,
    tile_send,
    tile_recv,
):
    dp = lax.axis_index("dp")
    me = lax.axis_index("tensor")
    z, b = me // 2, me % 2
    z_down, z_up = (z + 7) % 8, (z + 1) % 8
    partner = me + 1 - 2 * b
    target = {DOWN: z_up * 2 + b, UP: z_down * 2 + b, ACROSS: partner}

    def query_peer(r):
        d = (dp + r) % N
        other = (d // 8 + dp // 8) % 2
        return d, me + other * (1 - 2 * b)

    owners = [me]
    same = lambda d: ((z + d + 8) % 8) * 2 + b
    opposite = lambda d: ((z + d + 8) % 8) * 2 + 1 - b
    for trio in (
        (same(-1), same(1), opposite(0)),
        (same(-2), same(2), opposite(1)),
        (same(-3), same(3), opposite(2)),
        (same(-4), opposite(3), opposite(-2)),
        (opposite(-3), opposite(4), opposite(-1)),
    ):
        owners += trio

    load_x = pltpu.make_async_copy(inputs, x_rows, load_sem.at[0])
    load_pm = pltpu.make_async_copy(proj_model, pm, load_sem.at[1])
    load_own = pltpu.make_async_copy(cotangent, block.at[0, :, pl.ds(0, D)], load_sem.at[2])
    load_ph = pltpu.make_async_copy(proj_hidden, ph, load_sem.at[3])
    load_query = pltpu.make_async_copy(
        queries.at[:, pl.ds(pl.multiple_of(me * SLICE, 128), SLICE)],
        query_in.at[dp],
        load_sem.at[4],
    )
    load_weight = [
        pltpu.make_async_copy(
            down_weight.at[:, pl.ds(low, high - low)],
            weight.at[:, pl.ds(low, high - low)],
            load_sem.at[5 + j],
        )
        for j, (low, high) in enumerate(CUTS)
    ]
    load_gates = [
        pltpu.make_async_copy(
            gate_up.at[:, pl.ds(pl.multiple_of(owner * ROWS, ROWS), ROWS), :],
            gates.at[:, pl.ds(slot * ROWS, ROWS), :],
            gate_sem.at[slot],
        )
        for slot, owner in enumerate(owners)
    ]
    load_x.start()
    load_pm.start()
    load_own.start()
    load_ph.start()
    for copy in load_gates:
        copy.start()
    for copy in load_weight:
        copy.start()
    load_query.start()

    barrier = pltpu.get_barrier_semaphore()

    def greet(r, carry):
        pl.semaphore_signal(
            barrier, inc=1, device_id=(dp, (me + r) % N), device_id_type=MESH
        )
        pl.semaphore_signal(barrier, inc=1, device_id=query_peer(r), device_id_type=MESH)
        return carry

    lax.fori_loop(1, N, greet, 0)
    pl.semaphore_wait(barrier, 2 * (N - 1))

    def pass_on(step, link, piece, source=None):
        where = block.at[slot_of(step, link), :, span(piece)]
        return pltpu.make_async_remote_copy(
            src_ref=where if source is None else source,
            dst_ref=where,
            send_sem=send_sem.at[link, step - 1, piece],
            recv_sem=recv_sem.at[link, step - 1, piece],
            device_id=(dp, target[link]),
            device_id_type=MESH,
        )

    sent = []

    def send(step, link, piece, source_slot):
        copy = pass_on(step, link, piece, block.at[source_slot, :, span(piece)])
        copy.start()
        sent.append(copy)

    for link in (DOWN, UP, ACROSS):
        for piece in range(PIECES - 1):
            copy = pass_on(1, link, piece, cotangent.at[:, span(piece)])
            copy.start()
            sent.append(copy)

    load_x.wait()
    load_pm.wait()
    lead = dot(x_rows[...], pm[:, : 2 * RANK], (((1,), (0,)), ((), ())))
    load_own.wait()
    block[0, :, D:] = lead.astype(jnp.bfloat16)
    for link in (DOWN, UP, ACROSS):
        send(1, link, PIECES - 1, 0)

    def query_copy(r):
        d, tensor = query_peer(r)
        return pltpu.make_async_remote_copy(
            src_ref=queries.at[:, pl.ds(pl.multiple_of(tensor * SLICE, 128), SLICE)],
            dst_ref=query_in.at[dp],
            send_sem=query_send.at[r],
            recv_sem=query_recv.at[dp],
            device_id=(d, tensor),
            device_id_type=MESH,
        )

    def start_query(r, carry):
        query_copy(r).start()
        return carry

    lax.fori_loop(1, N, start_query, 0)

    load_ph.wait()
    for copy in load_gates:
        copy.wait()

    def gate_rows(i, carry):
        rows = pl.ds(pl.multiple_of(i * ROWS, ROWS), ROWS)
        g = gates[0, rows, :].astype(jnp.float32)
        u = gates[1, rows, :].astype(jnp.float32)
        s = jax.nn.sigmoid(g)
        silu = g * s
        factor_up[rows, :] = silu
        factor_gate[rows, :] = u * s * (1.0 + g * (1.0 - s))
        hidden = (silu * u).astype(jnp.bfloat16)
        hidden_proj[rows, :] = dot(hidden, ph[...], (((1,), (0,)), ((), ())))
        return carry

    lax.fori_loop(0, N, gate_rows, 0)
    total[...] = jnp.zeros_like(total)
    parts[...] = jnp.zeros_like(parts)

    live_count = lengths[0]

    def multiply(first, count, piece):
        low, high = CUTS[piece]
        rows = count * ROWS
        x = block[first : first + count, :, low:high].reshape(rows, high - low)
        for n in range(0, FF, 256):
            m = min(n + 256, FF)
            term = dot(x, weight[n:m, low:high], NT)
            if piece:
                term += grad[:rows, n:m]
            grad[:rows, n:m] = term
        term = dot(x, pm[low:high, :], (((1,), (0,)), ((), ())))
        if piece:
            term += model_cot[:rows, :]
        model_cot[:rows, :] = term

    def finish(first, count):
        rows = count * ROWS
        here = pl.ds(first * ROWS, rows)
        g = grad[:rows, :]
        grad_gate = (g * factor_gate[here, :]).astype(jnp.bfloat16)
        grad_up = (g * factor_up[here, :]).astype(jnp.bfloat16)
        out_gate = dot(grad_gate, ph[...], (((1,), (0,)), ((), ())))
        out_up = dot(grad_up, ph[...], (((1,), (0,)), ((), ())))
        lane = lax.broadcasted_iota(jnp.int32, (rows, 2 * RANK), 1)
        right = jnp.concatenate(
            [
                jnp.where(lane < RANK, out_gate[:, : 2 * RANK], out_up[:, : 2 * RANK]),
                model_cot[:rows, 2 * RANK :],
            ],
            axis=1,
        )
        lead = block[first : first + count, :, D:].reshape(rows, 2 * RANK)
        left = jnp.concatenate(
            [lead.astype(jnp.float32), hidden_proj[here, 2 * RANK :]], axis=1
        )
        row = lax.broadcasted_iota(jnp.int32, (ROWS, 3 * RANK), 0)
        live = jnp.concatenate(
            [
                (row + owners[slot] * ROWS < live_count).astype(jnp.float32)
                for slot in range(first, first + count)
            ],
            axis=0,
        )
        total[...] += lax.dot_general(
            left * live,
            right,
            TN,
            precision=lax.Precision.HIGHEST,
            preferred_element_type=jnp.float32,
        )

    onward = {
        (1, DOWN): [(2, DOWN, slot_of(1, DOWN))],
        (2, DOWN): [(3, DOWN, slot_of(2, DOWN))],
        (3, DOWN): [(4, DOWN, slot_of(3, DOWN))],
        (1, UP): [(2, UP, slot_of(1, UP)), (2, ACROSS, slot_of(1, UP))],
        (2, UP): [(3, UP, slot_of(2, UP)), (3, ACROSS, slot_of(2, UP))],
        (3, ACROSS): [(4, UP, slot_of(3, ACROSS)), (4, ACROSS, slot_of(2, DOWN))],
        (4, UP): [(5, UP, slot_of(4, UP))],
        (4, ACROSS): [(5, DOWN, slot_of(4, ACROSS)), (5, ACROSS, slot_of(1, DOWN))],
    }
    for step in range(1, STEPS + 1):
        first, count = (0, 4) if step == 1 else (slot_of(step, 0), 3)
        for piece in range(PIECES):
            for link in (DOWN, UP, ACROSS):
                pass_on(step, link, piece).wait_recv()
                for later, way, slot in onward.get((step, link), ()):
                    send(later, way, piece, slot)
            if step == 1:
                load_weight[piece].wait()
            multiply(first, count, piece)
        finish(first, count)

    lane = lax.broadcasted_iota(jnp.int32, (RANK, 2 * RANK), 1)
    for k in range(3):
        rows = slice(k * RANK, (k + 1) * RANK)
        if k < 2:
            mine = total[rows, : 2 * RANK]
        else:
            mine = jnp.concatenate([total[rows, 2 * RANK :]] * 2, axis=1)
        swapped = pltpu.roll(mine, RANK, 1)
        turned[0, rows, :] = mine if k != 1 else swapped
        turned[1, rows, :] = swapped if k != 1 else mine
    lane = lax.broadcasted_iota(jnp.int32, (6, 2 * RANK), 1)
    for t in range(N):
        even = turned[0, pl.ds(12 * t, 6, stride=2), :]
        odd = turned[1, pl.ds(12 * t + 1, 6, stride=2), :]
        parts[t, :6, :] = jnp.where(lane < RANK, even, odd)

    def parts_copy(r):
        t = (me + r) % N
        return pltpu.make_async_remote_copy(
            src_ref=parts.at[t],
            dst_ref=parts_in.at[me],
            send_sem=parts_send.at[r],
            recv_sem=parts_recv.at[me],
            device_id=(dp, t),
            device_id_type=MESH,
        )

    def start_parts(r, carry):
        parts_copy(r).start()
        return carry

    lax.fori_loop(1, N, start_parts, 0)
    parts_in[me] = parts[me]

    def arrival(ref, sems, index):
        return pltpu.make_async_remote_copy(
            src_ref=ref.at[index],
            dst_ref=ref.at[index],
            send_sem=sems.at[index],
            recv_sem=sems.at[index],
            device_id=(dp, partner),
            device_id_type=MESH,
        )

    load_query.wait()

    def wait_query(r, carry):
        arrival(query_in, query_recv, (dp + r) % N).wait_recv()
        return carry

    lax.fori_loop(1, N, wait_query, 0)

    def wait_parts(r, carry):
        arrival(parts_in, parts_recv, (me + r) % N).wait_recv()
        return carry

    lax.fori_loop(1, N, wait_parts, 0)

    entries = jnp.sum(parts_in[...], axis=0)
    squares = jnp.sum(entries * entries)
    flat = jnp.concatenate([entries[i : i + 1, :] for i in range(6)], axis=1)
    high = flat.astype(jnp.bfloat16).astype(jnp.float32)
    row = lax.broadcasted_iota(jnp.int32, (16, SLICE), 0)
    pair = jnp.where(row == 0, high, jnp.where(row == 1, flat - high, 0.0))
    products = dot(pair.astype(jnp.bfloat16), query_in[...].reshape(N * 16, SLICE), NT)
    scores = products[0:1, :] + products[1:2, :]
    row = lax.broadcasted_iota(jnp.int32, (8, 128), 0)
    tile[...] = jnp.where(
        row == 0, scores[:, :128], jnp.where(row == 1, scores[:, 128:], squares)
    )

    def tile_copy(r):
        return pltpu.make_async_remote_copy(
            src_ref=tile,
            dst_ref=tiles_in.at[me],
            send_sem=tile_send.at[r],
            recv_sem=tile_recv.at[me],
            device_id=(dp, (me + r) % N),
            device_id_type=MESH,
        )

    def start_tile(r, carry):
        tile_copy(r).start()
        return carry

    lax.fori_loop(1, N, start_tile, 0)
    tiles_in[me] = tile[...]

    for copy in sent:
        copy.wait_send()

    def wait_sends(r, carry):
        query_copy(r).wait_send()
        parts_copy(r).wait_send()
        return carry

    lax.fori_loop(1, N, wait_sends, 0)

    def wait_tiles(r, carry):
        arrival(tiles_in, tile_recv, (me + r) % N).wait_recv()
        return carry

    lax.fori_loop(1, N, wait_tiles, 0)
    summed = jnp.sum(tiles_in[...], axis=0)
    norm = jnp.sqrt(summed[2:3, :] + 1e-06)
    out[:, :128] = summed[0:1, :] / norm
    out[:, 128:] = summed[1:2, :] / norm

    def wait_tile_sends(r, carry):
        tile_copy(r).wait_send()
        return carry

    lax.fori_loop(1, N, wait_tile_sends, 0)


def per_device(inputs, cotangent, gate_up, down_weight, proj_model, proj_hidden, lengths, queries):
    anywhere = pl.BlockSpec(memory_space=pl.ANY)
    bf16, f32 = jnp.bfloat16, jnp.float32
    dma = pltpu.SemaphoreType.DMA
    return pl.pallas_call(
        kernel,
        out_shape=jax.ShapeDtypeStruct((1, N * 16), f32),
        in_specs=[pl.BlockSpec(memory_space=pltpu.SMEM)] + [anywhere] * 7,
        out_specs=pl.BlockSpec(memory_space=pltpu.VMEM),
        scratch_shapes=[
            pltpu.VMEM((N, ROWS, WIDE), bf16),
            pltpu.VMEM((FF, D), bf16),
            pltpu.VMEM((2, N * ROWS, FF), bf16),
            pltpu.VMEM((N * ROWS, FF), f32),
            pltpu.VMEM((N * ROWS, FF), f32),
            pltpu.VMEM((ROWS, D), bf16),
            pltpu.VMEM((D, 3 * RANK), bf16),
            pltpu.VMEM((FF, 3 * RANK), bf16),
            pltpu.VMEM((N * ROWS, 3 * RANK), f32),
            pltpu.VMEM((4 * ROWS, FF), f32),
            pltpu.VMEM((4 * ROWS, 3 * RANK), f32),
            pltpu.VMEM((3 * RANK, 3 * RANK), f32),
            pltpu.VMEM((2, 3 * RANK, 2 * RANK), f32),
            pltpu.VMEM((N, 8, 128), f32),
            pltpu.VMEM((N, 8, 128), f32),
            pltpu.VMEM((N, 16, SLICE), bf16),
            pltpu.VMEM((8, 128), f32),
            pltpu.VMEM((N, 8, 128), f32),
            dma((5 + PIECES,)),
            dma((N,)),
            dma((3, STEPS, PIECES)),
            dma((3, STEPS, PIECES)),
            dma((N,)),
            dma((N,)),
            dma((N,)),
            dma((N,)),
            dma((N,)),
            dma((N,)),
        ],
        compiler_params=pltpu.CompilerParams(
            collective_id=0, has_side_effects=True, vmem_limit_bytes=48 * 1024 * 1024
        ),
        cost_estimate=pl.CostEstimate(
            flops=4 * 10**9, bytes_accessed=12 * 10**6, transcendentals=10**6
        ),
    )(lengths, inputs, cotangent, gate_up, down_weight, proj_model, proj_hidden, queries)


def solution(mesh):
    return jax.shard_map(
        per_device,
        mesh=mesh,
        in_specs=(
            P(("dp", "tensor"), None),
            P(("dp", "tensor"), None),
            P(None, "dp", "tensor"),
            P("tensor", None),
            P(),
            P("tensor", None),
            P("dp"),
            P("dp", None),
        ),
        out_specs=P("dp", None),
        check_vma=False,
    )
```

time: 300 us -> 64.9 us (0.22)
  waiting for transfers between devices: 222 us -> 0 us
  Pallas kernels: 0 us -> 57.4 us
  blocking collectives: 35.9 us -> 0 us
  matrix products: 24.4 us -> 0 us
  between operations: 16.3 us -> 0.73 us
  local copies, waits for them, and re-layouts: 0.14 us -> 6.49 us
    psum x1 -> x0, waiting for transfers between devices: 119 us -> none  [per_device(): hidden_side = lax.psum(project_hidden(pieces, proj_hidden), 'tensor')]
    all_gather x2 -> x0, waiting for transfers between devices: 101 us -> none  [the longest x1 101 us: per_device(): lax.all_gather(cotangent, 'tensor', axis=0, tiled=True)]
    pallas_call x0 -> x1, Pallas kernels: none -> 57.4 us  [per_device(): pl.pallas_call(kernel, out_shape=jax.ShapeDtypeStruct((1, N * 16), f32),...]
    all_gather x1 -> x0, blocking collectives: 35.9 us -> none  [per_device(): model_all = lax.all_gather(model_side, 'tensor', axis=0, tiled=True)]
    dot_general x10 -> x0, matrix products: 24.4 us -> none  [the longest x2 15 us: contract_rows(): lax.dot_general(left, right, (((1,), (1,)), ((), ())), preferred_element_...]
    unnamed x10 -> x11, local copies, waits for them, and re-layouts: 0.04 us -> 6.49 us
  transfers between devices with their start and end apart: 3 -> 0, of which waited for: 2 -> 0; matrix products, arithmetic and copies ran while one was open for 3% -> 0% of each run, Pallas kernels for 0% -> 0%
where the time goes in v1:
time: 64.9 us; the launch traced here: 64.6 us
  Pallas kernels  57.4 us (88%)
  local copies, waits for them, and re-layouts  6.49 us (10%)
  between operations  0.73 us (1%)
    pallas_call x1, Pallas kernels, per_device(): pl.pallas_call(kernel, out_shape=jax.ShapeDtypeStruct((1, N * 16), f32),...  57.4 us
    unnamed x11, local copies, waits for them, and re-layouts  6.49 us

profile of v1, /device:TPU:2, one launch (start us, length us, event | category | flops | bytes accessed | tf_op | source)
XLA Modules:
  0.0 64.6 jit_solution(569023236138793518)
XLA Ops:
  0.7 0.0 copy-start.1
  0.7 0.0 copy-start.2
  0.7 0.0 copy-start.3
  0.7 1.3 %copy.10.proj_hidden = bf16[896,192]{1,0:T(8,128)(2,1)S(1)} copy(bf16[896,192]{0,1:T(8,128)(2,1)} %param.13) | data formatting | bytes 688128 | tf_op args[5]
  1.9 3.2 %copy.9.proj_model = bf16[4096,192]{1,0:T(8,128)(2,1)S(1)} copy(bf16[4096,192]{0,1:T(8,128)(2,1)} %param.12) | data formatting | bytes 3145728 | tf_op args[4]
  5.1 0.0 copy-done.1
  5.1 0.0 copy-done.2
  5.1 0.0 copy-done.3
  5.1 0.0 copy-start
  5.2 1.5 %copy-done = bf16[2,512,896]{2,1,0:T(8,128)(2,1)S(1)} copy-done((bf16[2,512,896]{2,1,0:T(8,128)(2,1)S(1)}, bf16[2,512,896]{2,1,0:T(8,128)(2,1)}, u32[]{:S(2)}) %copy-start) | copy-done | bytes 1835032
  6.6 57.4 %shard_map.82 = f32[1,256]{1,0:T(1,128)S(1)} custom-call(s32[1]{0:T(128)S(6)} %copy.12.lengths, bf16[32,4096]{1,0:T(8,128)(2,1)S(1)} %copy-done.2, bf16[32,4096]{1,0:T(8,128)(2,1)S(1)} %copy-done.3, bf16[2,512,896]{2,1,0:T(8,128)(2,1)S(1)} %copy-done, bf16[896,4096]{1,0:T(8,128)(2,1)} %down_weight.1, bf16[4096,192]{1,0:T(8,128)(2,1)S(1)} %copy.9.proj_model, ...), custom_call_target="tpu_custom_call" | custom-call | flops 4000000000 | bytes 12000000 | tf_op jit(solution)/shard_map/pallas_call | solution.py:411
  64.0 0.6 copy.13
Async XLA Ops:
  0.7 4.5 %copy-start.1 = (bf16[16,12288]{1,0:T(8,128)(2,1)S(1)}, bf16[16,12288]{1,0:T(8,128)(2,1)}, u32[]{:S(2)}) copy-start(bf16[16,12288]{1,0:T(8,128)(2,1)} %queries.1) | copy-start | bytes 1179652
  0.7 4.5 %copy-start.2 = (bf16[32,4096]{1,0:T(8,128)(2,1)S(1)}, bf16[32,4096]{1,0:T(8,128)(2,1)}, u32[]{:S(2)}) copy-start(bf16[32,4096]{1,0:T(8,128)(2,1)} %inputs.1) | copy-start | bytes 786436
  0.7 4.5 %copy-start.3 = (bf16[32,4096]{1,0:T(8,128)(2,1)S(1)}, bf16[32,4096]{1,0:T(8,128)(2,1)}, u32[]{:S(2)}) copy-start(bf16[32,4096]{1,0:T(8,128)(2,1)} %cotangent.1) | copy-start | bytes 786436
  5.1 1.5 %copy-start = (bf16[2,512,896]{2,1,0:T(8,128)(2,1)S(1)}, bf16[2,512,896]{2,1,0:T(8,128)(2,1)}, u32[]{:S(2)}) copy-start(bf16[2,512,896]{2,1,0:T(8,128)(2,1)} %gate_up.1) | copy-start | bytes 5505028

commit v2 on v1

v2 whole, which is shorter than its diff:
```python
import jax
import jax.numpy as jnp
from jax import lax
from jax.experimental import pallas as pl
from jax.experimental.pallas import tpu as pltpu
from jax.sharding import PartitionSpec as P

MESH = pl.DeviceIdType.MESH
RANK = 64
N = 16
STEPS = 5
PIECES = 2
D = 4096
FF = 896
ROWS = 32
WIDE = D + 2 * RANK
SLICE = 768
CUTS = tuple((D // PIECES * j, D // PIECES * (j + 1)) for j in range(PIECES))
NT = (((1,), (1,)), ((), ()))
OTHERS = [(4, 1), (4, 0)]
for far in (3, 2, 1):
    OTHERS += [(far, 1), (8 - far, 1), (far, 0), (8 - far, 0)]
OTHERS += [(0, 1)]

DOWN, UP, ACROSS = 0, 1, 2


def span(piece):
    low, high = CUTS[piece]
    return pl.ds(low, (WIDE if piece == PIECES - 1 else high) - low)


def slot_of(step, link):
    return 1 + 3 * (step - 1) + link


def dot(a, b, dims):
    return lax.dot_general(a, b, dims, preferred_element_type=jnp.float32)


def kernel(
    lengths,
    inputs,
    cotangent,
    gate_up,
    down_weight,
    proj_model,
    proj_hidden,
    queries,
    out,
    block,
    weight,
    gates,
    factor_up,
    factor_gate,
    x_rows,
    pm,
    ph,
    hidden_proj,
    grad,
    total,
    turned,
    parts,
    parts_in,
    query_in,
    tile,
    tiles_in,
    length,
    load_sem,
    gate_sem,
    send_sem,
    recv_sem,
    query_send,
    query_recv,
    parts_send,
    parts_recv,
    tile_send,
    tile_recv,
):
    dp = lax.axis_index("dp")
    me = lax.axis_index("tensor")
    z, b = me // 2, me % 2
    z_down, z_up = (z + 7) % 8, (z + 1) % 8
    partner = me + 1 - 2 * b
    target = {DOWN: z_up * 2 + b, UP: z_down * 2 + b, ACROSS: partner}

    y_hi, x, core = dp // 8, (dp // 2) % 4, dp % 2
    at = lambda y_hi, x, core: y_hi * 8 + x * 2 + core
    across = (at(1 - y_hi, x, core), partner)
    beside = (at(y_hi, x, 1 - core), me)
    x_up = (at(y_hi, (x + 1) % 4, core), me)
    x_down = (at(y_hi, (x + 3) % 4, core), me)

    owners = [me]
    same = lambda d: ((z + d + 8) % 8) * 2 + b
    opposite = lambda d: ((z + d + 8) % 8) * 2 + 1 - b
    for trio in (
        (same(-1), same(1), opposite(0)),
        (same(-2), same(2), opposite(1)),
        (same(-3), same(3), opposite(2)),
        (same(-4), opposite(3), opposite(-2)),
        (opposite(-3), opposite(4), opposite(-1)),
    ):
        owners += trio

    load_x = pltpu.make_async_copy(inputs, x_rows, load_sem.at[0])
    load_pm = pltpu.make_async_copy(proj_model.at[: 2 * RANK], pm, load_sem.at[1])
    load_last = pltpu.make_async_copy(
        proj_model.at[2 * RANK :], weight.at[FF:], load_sem.at[5 + PIECES]
    )
    load_own = pltpu.make_async_copy(cotangent, block.at[0, :, pl.ds(0, D)], load_sem.at[2])
    load_ph = pltpu.make_async_copy(proj_hidden, ph, load_sem.at[3])
    load_query = pltpu.make_async_copy(
        queries.at[:, pl.ds(pl.multiple_of(me * SLICE, 128), SLICE)],
        query_in.at[y_hi, x, core],
        load_sem.at[4],
    )
    load_weight = [
        pltpu.make_async_copy(
            down_weight.at[:, pl.ds(low, high - low)],
            weight.at[:FF, pl.ds(low, high - low)],
            load_sem.at[5 + j],
        )
        for j, (low, high) in enumerate(CUTS)
    ]
    load_gates = [
        pltpu.make_async_copy(
            gate_up.at[:, pl.ds(pl.multiple_of(owner * ROWS, ROWS), ROWS), :],
            gates.at[:, pl.ds(slot * ROWS, ROWS), :],
            gate_sem.at[slot],
        )
        for slot, owner in enumerate(owners)
    ]
    load_lengths = pltpu.make_async_copy(lengths, length, load_sem.at[6 + PIECES])
    load_lengths.start()
    load_x.start()
    load_pm.start()
    load_own.start()
    load_ph.start()
    for copy in load_gates:
        copy.start()
    load_last.start()
    for copy in load_weight:
        copy.start()
    load_query.start()

    barrier = pltpu.get_barrier_semaphore()

    for peer in [(dp, t) for t in target.values()] + [across, beside, x_up, x_down]:
        pl.semaphore_signal(barrier, inc=1, device_id=peer, device_id_type=MESH)
    pl.semaphore_wait(barrier, 7)

    def pass_on(step, link, piece, source=None):
        where = block.at[slot_of(step, link), :, span(piece)]
        return pltpu.make_async_remote_copy(
            src_ref=where if source is None else source,
            dst_ref=where,
            send_sem=send_sem.at[link, step - 1, piece],
            recv_sem=recv_sem.at[link, step - 1, piece],
            device_id=(dp, target[link]),
            device_id_type=MESH,
        )

    sent = []

    def send(step, link, piece, source_slot):
        copy = pass_on(step, link, piece, block.at[source_slot, :, span(piece)])
        copy.start()
        sent.append(copy)

    for link in (DOWN, UP, ACROSS):
        for piece in range(PIECES - 1):
            copy = pass_on(1, link, piece, cotangent.at[:, span(piece)])
            copy.start()
            sent.append(copy)

    load_x.wait()
    load_pm.wait()
    lead = dot(x_rows[...], pm[...], NT)
    load_own.wait()
    block[0, :, D:] = lead.astype(jnp.bfloat16)
    for link in (DOWN, UP, ACROSS):
        send(1, link, PIECES - 1, 0)

    def query_copy(source, slot, stage, peer):
        return pltpu.make_async_remote_copy(
            src_ref=source,
            dst_ref=query_in.at[slot],
            send_sem=query_send.at[stage],
            recv_sem=query_recv.at[stage],
            device_id=peer,
            device_id_type=MESH,
        )

    both = slice(None)
    x_before, x_after = (x + 3) % 4, (x + 1) % 4
    slots = [(y_hi, x, core), (both, x, core), (both, x), (both, x), (both, x_before)]
    arriving = [
        (1 - y_hi, x, core),
        (both, x, 1 - core),
        (both, x_before),
        (both, x_after),
        (both, (x + 2) % 4),
    ]
    peers = [across, beside, x_up, x_down, x_up]

    def send_queries(stage):
        if stage:
            source = query_in.at[slots[stage]]
        else:
            source = queries.at[:, pl.ds(pl.multiple_of(partner * SLICE, 128), SLICE)]
        copy = query_copy(source, slots[stage], stage, peers[stage])
        copy.start()
        sent.append(copy)

    def wait_queries(stage):
        here = query_in.at[arriving[stage]]
        query_copy(here, arriving[stage], stage, peers[stage]).wait_recv()

    send_queries(0)

    load_ph.wait()

    def gate_rows(i, carry):
        rows = pl.ds(pl.multiple_of(i * ROWS, ROWS), ROWS)
        g = gates[0, rows, :].astype(jnp.float32)
        u = gates[1, rows, :].astype(jnp.float32)
        s = jax.nn.sigmoid(g)
        silu = g * s
        factor_up[rows, :] = silu
        factor_gate[rows, :] = u * s * (1.0 + g * (1.0 - s))
        hidden = (silu * u).astype(jnp.bfloat16)
        hidden_proj[rows, :] = dot(hidden, ph[2 * RANK :, :], NT)
        return carry

    total[...] = jnp.zeros_like(total)
    parts[...] = jnp.zeros_like(parts)
    load_lengths.wait()
    live_count = length[0]

    def multiply(first, count, piece):
        low, high = CUTS[piece]
        rows = count * ROWS
        x = block[first : first + count, :, low:high].reshape(rows, high - low)
        for n in range(0, FF + RANK, 256):
            m = min(n + 256, FF + RANK)
            term = dot(x, weight[n:m, low:high], NT)
            if piece:
                term += grad[:rows, n:m]
            grad[:rows, n:m] = term

    def finish(first, count):
        rows = count * ROWS
        here = pl.ds(first * ROWS, rows)
        g = grad[:rows, :FF]
        grad_gate = (g * factor_gate[here, :]).astype(jnp.bfloat16)
        grad_up = (g * factor_up[here, :]).astype(jnp.bfloat16)
        lead = block[first : first + count, :, D:].reshape(rows, 2 * RANK)
        left = jnp.concatenate(
            [lead.astype(jnp.float32), hidden_proj[here, :]], axis=1
        )
        row = lax.broadcasted_iota(jnp.int32, (ROWS, 3 * RANK), 0)
        live = jnp.concatenate(
            [
                (row + owners[slot] * ROWS < live_count).astype(jnp.float32)
                for slot in range(first, first + count)
            ],
            axis=0,
        )
        left = (left * live).T
        rights = (
            dot(grad_gate, ph[:RANK, :], NT),
            dot(grad_up, ph[RANK : 2 * RANK, :], NT),
            grad[:rows, FF:],
        )
        for k, right in enumerate(rights):
            rows = slice(k * RANK, (k + 1) * RANK)
            total[rows, :] += jnp.dot(
                left[rows, :],
                right,
                precision=lax.Precision.HIGHEST,
                preferred_element_type=jnp.float32,
            )

    onward = {
        (1, DOWN): [(2, DOWN, slot_of(1, DOWN))],
        (2, DOWN): [(3, DOWN, slot_of(2, DOWN))],
        (3, DOWN): [(4, DOWN, slot_of(3, DOWN))],
        (1, UP): [(2, UP, slot_of(1, UP)), (2, ACROSS, slot_of(1, UP))],
        (2, UP): [(3, UP, slot_of(2, UP)), (3, ACROSS, slot_of(2, UP))],
        (3, ACROSS): [(4, UP, slot_of(3, ACROSS)), (4, ACROSS, slot_of(2, DOWN))],
        (4, UP): [(5, UP, slot_of(4, UP))],
        (4, ACROSS): [(5, DOWN, slot_of(4, ACROSS)), (5, ACROSS, slot_of(1, DOWN))],
    }
    for step in range(1, STEPS + 1):
        first, count = (0, 4) if step == 1 else (slot_of(step, 0), 3)
        for piece in range(PIECES):
            for link in (DOWN, UP, ACROSS):
                pass_on(step, link, piece).wait_recv()
                for later, way, slot in onward.get((step, link), ()):
                    send(later, way, piece, slot)
            if step == 1:
                if not piece:
                    load_last.wait()
                load_weight[piece].wait()
            multiply(first, count, piece)
            if not piece:
                for slot in range(first, first + count):
                    load_gates[slot].wait()
                lax.fori_loop(first, first + count, gate_rows, 0)
        if step == 1:
            load_query.wait()
            wait_queries(0)
            send_queries(1)
        if step == 2:
            wait_queries(1)
            send_queries(2)
            send_queries(3)
        if step == 3:
            wait_queries(2)
            send_queries(4)
        if step == 4:
            wait_queries(3)
            wait_queries(4)
        finish(first, count)

    turned[...] = jnp.concatenate([total[...], total[...]], axis=1)
    lane = lax.broadcasted_iota(jnp.int32, (6, 2 * RANK), 1)
    for t in range(N):
        even = turned[pl.ds(12 * t, 6, stride=2), :]
        odd = turned[pl.ds(12 * t + 1, 6, stride=2), :]
        parts[t, :6, :] = jnp.where(lane < RANK, even, odd)

    def other(r):
        far, over = OTHERS[r]
        return (z + far) % 8 * 2 + (1 - b if over else b)

    def exchange(source, target, sends, recvs):
        copies = []
        for r in range(N - 1):
            copy = pltpu.make_async_remote_copy(
                src_ref=source(other(r)),
                dst_ref=target(r),
                send_sem=sends.at[r],
                recv_sem=recvs.at[r],
                device_id=(dp, other(r)),
                device_id_type=MESH,
            )
            copy.start()
            copies.append(copy)
        return copies

    to_sum = exchange(
        lambda t: parts.at[t], lambda r: parts_in.at[r], parts_send, parts_recv
    )
    parts_in[N - 1] = parts[me]
    for copy in to_sum:
        copy.wait_recv()

    entries = jnp.sum(parts_in[...], axis=0)
    squares = jnp.sum(entries * entries)
    flat = jnp.concatenate([entries[i : i + 1, :] for i in range(6)], axis=1)
    high = flat.astype(jnp.bfloat16).astype(jnp.float32)
    row = lax.broadcasted_iota(jnp.int32, (16, SLICE), 0)
    pair = jnp.where(row == 0, high, jnp.where(row == 1, flat - high, 0.0))
    products = dot(pair.astype(jnp.bfloat16), query_in[...].reshape(N * 16, SLICE), NT)
    scores = products[0:1, :] + products[1:2, :]
    row = lax.broadcasted_iota(jnp.int32, (8, 128), 0)
    tile[...] = jnp.where(
        row == 0, scores[:, :128], jnp.where(row == 1, scores[:, 128:], squares)
    )

    to_add = exchange(
        lambda t: tile, lambda r: tiles_in.at[me], tile_send, tile_recv
    )
    tiles_in[me] = tile[...]
    for copy in sent + to_sum:
        copy.wait_send()
    for copy in to_add:
        copy.wait_recv()
    summed = jnp.sum(tiles_in[...], axis=0)
    norm = jnp.sqrt(summed[2:3, :] + 1e-06)
    out[:, :128] = summed[0:1, :] / norm
    out[:, 128:] = summed[1:2, :] / norm

    for copy in to_add:
        copy.wait_send()


def per_device(inputs, cotangent, gate_up, down_weight, proj_model, proj_hidden, lengths, queries):
    anywhere = pl.BlockSpec(memory_space=pl.ANY)
    bf16, f32 = jnp.bfloat16, jnp.float32
    dma = pltpu.SemaphoreType.DMA
    return pl.pallas_call(
        kernel,
        out_shape=jax.ShapeDtypeStruct((1, N * 16), f32),
        in_specs=[anywhere] * 8,
        out_specs=pl.BlockSpec(memory_space=pltpu.VMEM),
        scratch_shapes=[
            pltpu.VMEM((N, ROWS, WIDE), bf16),
            pltpu.VMEM((FF + RANK, D), bf16),
            pltpu.VMEM((2, N * ROWS, FF), bf16),
            pltpu.VMEM((N * ROWS, FF), f32),
            pltpu.VMEM((N * ROWS, FF), f32),
            pltpu.VMEM((ROWS, D), bf16),
            pltpu.VMEM((2 * RANK, D), bf16),
            pltpu.VMEM((3 * RANK, FF), bf16),
            pltpu.VMEM((N * ROWS, RANK), f32),
            pltpu.VMEM((4 * ROWS, FF + RANK), f32),
            pltpu.VMEM((3 * RANK, RANK), f32),
            pltpu.VMEM((3 * RANK, 2 * RANK), f32),
            pltpu.VMEM((N, 8, 128), f32),
            pltpu.VMEM((N, 8, 128), f32),
            pltpu.VMEM((2, 4, 2, 16, SLICE), bf16),
            pltpu.VMEM((8, 128), f32),
            pltpu.VMEM((N, 8, 128), f32),
            pltpu.SMEM((1,), jnp.int32),
            dma((7 + PIECES,)),
            dma((N,)),
            dma((3, STEPS, PIECES)),
            dma((3, STEPS, PIECES)),
            dma((5,)),
            dma((5,)),
            dma((N,)),
            dma((N,)),
            dma((N,)),
            dma((N,)),
        ],
        compiler_params=pltpu.CompilerParams(
            collective_id=0, has_side_effects=True, vmem_limit_bytes=54 * 1024 * 1024
        ),
        cost_estimate=pl.CostEstimate(
            flops=4 * 10**9, bytes_accessed=12 * 10**6, transcendentals=10**6
        ),
    )(lengths, inputs, cotangent, gate_up, down_weight, proj_model.T, proj_hidden.T, queries)


def solution(mesh):
    return jax.shard_map(
        per_device,
        mesh=mesh,
        in_specs=(
            P(("dp", "tensor"), None),
            P(("dp", "tensor"), None),
            P(None, "dp", "tensor"),
            P("tensor", None),
            P(),
            P("tensor", None),
            P("dp"),
            P("dp", None),
        ),
        out_specs=P("dp", None),
        check_vma=False,
    )
```

time: 64.9 us -> 55.4 us (0.85)
  local copies, waits for them, and re-layouts: 6.49 us -> 1.24 us
  Pallas kernels: 57.4 us -> 53.4 us
    unnamed x11 -> x1, local copies, waits for them, and re-layouts: 6.49 us -> 1.24 us
    pallas_call x1, Pallas kernels: 57.4 us -> 53.4 us  [per_device(): pl.pallas_call(kernel, out_shape=jax.ShapeDtypeStruct((1, N * 16), f32),...]
where the time goes in v2:
time: 55.4 us; the launch traced here: 55.3 us
  Pallas kernels  53.4 us (96%)
  local copies, waits for them, and re-layouts  1.24 us (2%)
  between operations  0.66 us (1%)
    pallas_call x1, Pallas kernels, per_device(): pl.pallas_call(kernel, out_shape=jax.ShapeDtypeStruct((1, N * 16), f32),...  53.4 us
    unnamed x1, local copies, waits for them, and re-layouts  1.24 us

profile of v2, /device:TPU:2, one launch (start us, length us, event | category | flops | bytes accessed | tf_op | source)
XLA Modules:
  0.0 55.3 jit_solution(7257274601322650481)
XLA Ops:
  0.7 53.4 %shard_map.82 = f32[1,256]{1,0:T(1,128)} custom-call(s32[1]{0:T(128)S(6)} %copy.10.lengths, bf16[32,4096]{1,0:T(8,128)(2,1)} %inputs.1, bf16[32,4096]{1,0:T(8,128)(2,1)} %cotangent.1, bf16[2,512,896]{2,1,0:T(8,128)(2,1)} %gate_up.1, bf16[896,4096]{1,0:T(8,128)(2,1)} %down_weight.1, bf16[192,4096]{1,0:T(8,128)(2,1)} %bitcast.2, bf16[192,896]{1,0:T(8,128)(2,1)} %bitcast.3, ...), custom_call_target="tpu_custom_call" | custom-call | flops 4000000000 | bytes 12000000 | tf_op jit(solution)/shard_map/pallas_call | solution.py:394
  54.1 1.2 %copy.11 = f32[1,256]{1,0:T(1,128)} copy(f32[1,256]{1,0:T(1,128)} %shard_map.82) | data formatting | bytes 2048

commit v3 on v2

--- a/solution.py
+++ b/solution.py
@@ -9,13 +9,15 @@
 RANK = 64
 N = 16
 STEPS = 5
-PIECES = 2
+PIECES = 3
 D = 4096
 FF = 896
 ROWS = 32
 WIDE = D + 2 * RANK
 SLICE = 768
-CUTS = tuple((D // PIECES * j, D // PIECES * (j + 1)) for j in range(PIECES))
+CUTS = ((0, 1408), (1408, 2816), (2816, D))
+LEAD = CUTS[-1][0]
+SHIFT = (0, 0, 2 * RANK)
 NT = (((1,), (1,)), ((), ()))
 OTHERS = [(4, 1), (4, 0)]
 for far in (3, 2, 1):
@@ -27,7 +29,9 @@
 
 def span(piece):
     low, high = CUTS[piece]
-    return pl.ds(low, (WIDE if piece == PIECES - 1 else high) - low)
+    if piece == PIECES - 2:
+        high += 2 * RANK
+    return pl.ds(low + SHIFT[piece], high - low)
 
 
 def slot_of(step, link):
@@ -58,6 +62,7 @@
     ph,
     hidden_proj,
     grad,
+    sources,
     total,
     turned,
     parts,
@@ -108,7 +113,14 @@
     load_last = pltpu.make_async_copy(
         proj_model.at[2 * RANK :], weight.at[FF:], load_sem.at[5 + PIECES]
     )
-    load_own = pltpu.make_async_copy(cotangent, block.at[0, :, pl.ds(0, D)], load_sem.at[2])
+    load_own = [
+        pltpu.make_async_copy(
+            cotangent.at[:, pl.ds(low, high - low)],
+            block.at[0, :, pl.ds(at, high - low)],
+            load_sem.at[sem],
+        )
+        for low, high, at, sem in ((0, LEAD, 0, 2), (LEAD, D, LEAD + 2 * RANK, 7 + PIECES))
+    ]
     load_ph = pltpu.make_async_copy(proj_hidden, ph, load_sem.at[3])
     load_query = pltpu.make_async_copy(
         queries.at[:, pl.ds(pl.multiple_of(me * SLICE, 128), SLICE)],
@@ -132,22 +144,14 @@
         for slot, owner in enumerate(owners)
     ]
     load_lengths = pltpu.make_async_copy(lengths, length, load_sem.at[6 + PIECES])
-    load_lengths.start()
+
+    barrier = pltpu.get_barrier_semaphore()
+    for peer in [(dp, t) for t in target.values()] + [across, beside, x_up, x_down]:
+        pl.semaphore_signal(barrier, inc=1, device_id=peer, device_id_type=MESH)
     load_x.start()
     load_pm.start()
-    load_own.start()
-    load_ph.start()
-    for copy in load_gates:
+    for copy in load_own:
         copy.start()
-    load_last.start()
-    for copy in load_weight:
-        copy.start()
-    load_query.start()
-
-    barrier = pltpu.get_barrier_semaphore()
-
-    for peer in [(dp, t) for t in target.values()] + [across, beside, x_up, x_down]:
-        pl.semaphore_signal(barrier, inc=1, device_id=peer, device_id_type=MESH)
     pl.semaphore_wait(barrier, 7)
 
     def pass_on(step, link, piece, source=None):
@@ -168,19 +172,38 @@
         copy.start()
         sent.append(copy)
 
-    for link in (DOWN, UP, ACROSS):
-        for piece in range(PIECES - 1):
-            copy = pass_on(1, link, piece, cotangent.at[:, span(piece)])
-            copy.start()
-            sent.append(copy)
-
+    first_sends = [
+        pass_on(1, link, piece, cotangent.at[:, span(piece)])
+        for piece in range(PIECES - 2)
+        for link in (DOWN, UP, ACROSS)
+    ]
+    sent += first_sends
+
+    def send_first(turn):
+        @pl.when(core == turn)
+        def _():
+            for copy in first_sends:
+                copy.start()
+
+    send_first(0)
+    load_ph.start()
+    load_lengths.start()
+    for copy in load_gates:
+        copy.start()
+    load_last.start()
+    for copy in load_weight:
+        copy.start()
+    load_query.start()
     load_x.wait()
+    send_first(1)
     load_pm.wait()
     lead = dot(x_rows[...], pm[...], NT)
-    load_own.wait()
-    block[0, :, D:] = lead.astype(jnp.bfloat16)
-    for link in (DOWN, UP, ACROSS):
-        send(1, link, PIECES - 1, 0)
+    for copy in load_own:
+        copy.wait()
+    block[0, :, LEAD : LEAD + 2 * RANK] = lead.astype(jnp.bfloat16)
+    for piece in (PIECES - 2, PIECES - 1):
+        for link in (DOWN, UP, ACROSS):
+            send(1, link, piece, 0)
 
     def query_copy(source, slot, stage, peer):
         return pltpu.make_async_remote_copy(
@@ -241,7 +264,8 @@
     def multiply(first, count, piece):
         low, high = CUTS[piece]
         rows = count * ROWS
-        x = block[first : first + count, :, low:high].reshape(rows, high - low)
+        at = low + SHIFT[piece]
+        x = block[first : first + count, :, at : at + high - low].reshape(rows, high - low)
         for n in range(0, FF + RANK, 256):
             m = min(n + 256, FF + RANK)
             term = dot(x, weight[n:m, low:high], NT)
@@ -249,16 +273,10 @@
                 term += grad[:rows, n:m]
             grad[:rows, n:m] = term
 
-    def finish(first, count):
+    def prepare(first, count):
         rows = count * ROWS
         here = pl.ds(first * ROWS, rows)
-        g = grad[:rows, :FF]
-        grad_gate = (g * factor_gate[here, :]).astype(jnp.bfloat16)
-        grad_up = (g * factor_up[here, :]).astype(jnp.bfloat16)
-        lead = block[first : first + count, :, D:].reshape(rows, 2 * RANK)
-        left = jnp.concatenate(
-            [lead.astype(jnp.float32), hidden_proj[here, :]], axis=1
-        )
+        lead = block[first : first + count, :, LEAD : LEAD + 2 * RANK].reshape(rows, 2 * RANK)
         row = lax.broadcasted_iota(jnp.int32, (ROWS, 3 * RANK), 0)
         live = jnp.concatenate(
             [
@@ -267,20 +285,27 @@
             ],
             axis=0,
         )
-        left = (left * live).T
-        rights = (
-            dot(grad_gate, ph[:RANK, :], NT),
-            dot(grad_up, ph[RANK : 2 * RANK, :], NT),
-            grad[:rows, FF:],
-        )
-        for k, right in enumerate(rights):
-            rows = slice(k * RANK, (k + 1) * RANK)
-            total[rows, :] += jnp.dot(
-                left[rows, :],
-                right,
-                precision=lax.Precision.HIGHEST,
-                preferred_element_type=jnp.float32,
-            )
+        left = jnp.concatenate([lead.astype(jnp.float32), hidden_proj[here, :]], axis=1)
+        sources[:, :rows] = (left * live).T
+
+    def split(a):
+        high = a.astype(jnp.bfloat16)
+        return high, (a - high.astype(jnp.float32)).astype(jnp.bfloat16)
+
+    def finish(first, count):
+        rows = count * ROWS
+        here = pl.ds(first * ROWS, rows)
+        nn = (((1,), (0,)), ((), ()))
+        source, source_low = split(sources[2 * RANK :, :rows])
+        target, target_low = split(grad[:rows, FF:])
+        last = dot(source, target, nn) + dot(source, target_low, nn)
+        total[2 * RANK :, :] += last + dot(source_low, target, nn)
+        for k, factor in enumerate((factor_gate, factor_up)):
+            columns = slice(k * RANK, (k + 1) * RANK)
+            moved = (grad[:rows, :FF] * factor[here, :]).astype(jnp.bfloat16)
+            target, target_low = split(dot(moved, ph[columns, :], NT))
+            source = sources[columns, :rows].astype(jnp.bfloat16)
+            total[columns, :] += dot(source, target, nn) + dot(source, target_low, nn)
 
     onward = {
         (1, DOWN): [(2, DOWN, slot_of(1, DOWN))],
@@ -308,6 +333,8 @@
                 for slot in range(first, first + count):
                     load_gates[slot].wait()
                 lax.fori_loop(first, first + count, gate_rows, 0)
+            if piece == PIECES - 2:
+                prepare(first, count)
         if step == 1:
             load_query.wait()
             wait_queries(0)
@@ -407,6 +434,7 @@
             pltpu.VMEM((3 * RANK, FF), bf16),
             pltpu.VMEM((N * ROWS, RANK), f32),
             pltpu.VMEM((4 * ROWS, FF + RANK), f32),
+            pltpu.VMEM((3 * RANK, 4 * ROWS), f32),
             pltpu.VMEM((3 * RANK, RANK), f32),
             pltpu.VMEM((3 * RANK, 2 * RANK), f32),
             pltpu.VMEM((N, 8, 128), f32),
@@ -415,7 +443,7 @@
             pltpu.VMEM((8, 128), f32),
             pltpu.VMEM((N, 8, 128), f32),
             pltpu.SMEM((1,), jnp.int32),
-            dma((7 + PIECES,)),
+            dma((8 + PIECES,)),
             dma((N,)),
             dma((3, STEPS, PIECES)),
             dma((3, STEPS, PIECES)),
@@ -427,7 +455,7 @@
             dma((N,)),
         ],
         compiler_params=pltpu.CompilerParams(
-            collective_id=0, has_side_effects=True, vmem_limit_bytes=54 * 1024 * 1024
+            collective_id=0, has_side_effects=True, vmem_limit_bytes=55091 * 1024
         ),
         cost_estimate=pl.CostEstimate(
             flops=4 * 10**9, bytes_accessed=12 * 10**6, transcendentals=10**6

time: 55.4 us -> 53.8 us (0.971)
  Pallas kernels: 53.4 us -> 52.5 us
  local copies, waits for them, and re-layouts: 1.24 us -> 0.56 us
    pallas_call x1, Pallas kernels: 53.4 us -> 52.5 us  [per_device(): pl.pallas_call(kernel, out_shape=jax.ShapeDtypeStruct((1, N * 16), f32),...]
    unnamed x1, local copies, waits for them, and re-layouts: 1.24 us -> 0.56 us
where the time goes in v3:
time: 53.8 us
  Pallas kernels  52.5 us (98%)
  between operations  0.66 us (1%)
  local copies, waits for them, and re-layouts  0.56 us (1%)
    pallas_call x1, Pallas kernels, per_device(): pl.pallas_call(kernel, out_shape=jax.ShapeDtypeStruct((1, N * 16), f32),...  52.5 us

profile of v3, /device:TPU:2, one launch (start us, length us, event | category | flops | bytes accessed | tf_op | source)
XLA Modules:
  0.0 53.8 jit_solution(11051592977716128417)
XLA Ops:
  0.7 52.5 %shard_map.82 = f32[1,256]{1,0:T(1,128)S(1)} custom-call(s32[1]{0:T(128)S(6)} %copy.10.lengths, bf16[32,4096]{1,0:T(8,128)(2,1)} %inputs.1, bf16[32,4096]{1,0:T(8,128)(2,1)} %cotangent.1, bf16[2,512,896]{2,1,0:T(8,128)(2,1)} %gate_up.1, bf16[896,4096]{1,0:T(8,128)(2,1)} %down_weight.1, bf16[192,4096]{1,0:T(8,128)(2,1)} %bitcast.2, bf16[192,896]{1,0:T(8,128)(2,1)} %bitcast.3, ...), custom_call_target="tpu_custom_call" | custom-call | flops 4000000000 | bytes 12000000 | tf_op jit(solution)/shard_map/pallas_call | solution.py:421
  53.2 0.6 %copy.11 = f32[1,256]{1,0:T(1,128)} copy(f32[1,256]{1,0:T(1,128)S(1)} %shard_map.82) | data formatting | bytes 2048

commit v4 on v3

--- a/solution.py
+++ b/solution.py
@@ -14,7 +14,9 @@
 FF = 896
 ROWS = 32
 WIDE = D + 2 * RANK
-SLICE = 768
+SLICES = 8
+SLICE = 1536
+LINES = SLICE // 128
 CUTS = ((0, 1408), (1408, 2816), (2816, D))
 LEAD = CUTS[-1][0]
 SHIFT = (0, 0, 2 * RANK)
@@ -23,6 +25,7 @@
 for far in (3, 2, 1):
     OTHERS += [(far, 1), (8 - far, 1), (far, 0), (8 - far, 0)]
 OTHERS += [(0, 1)]
+NEAREST = [(2, 1), (2, 0), (7, 1), (1, 1), (7, 0), (1, 0), (0, 1)]
 
 DOWN, UP, ACROSS = 0, 1, 2
 
@@ -87,6 +90,8 @@
     z, b = me // 2, me % 2
     z_down, z_up = (z + 7) % 8, (z + 1) % 8
     partner = me + 1 - 2 * b
+    slice_of = lambda z, b: z % 4 * 2 + b
+    my_slice = slice_of(z, b)
     target = {DOWN: z_up * 2 + b, UP: z_down * 2 + b, ACROSS: partner}
 
     y_hi, x, core = dp // 8, (dp // 2) % 4, dp % 2
@@ -123,7 +128,7 @@
     ]
     load_ph = pltpu.make_async_copy(proj_hidden, ph, load_sem.at[3])
     load_query = pltpu.make_async_copy(
-        queries.at[:, pl.ds(pl.multiple_of(me * SLICE, 128), SLICE)],
+        queries.at[:, pl.ds(pl.multiple_of(my_slice * SLICE, 128), SLICE)],
         query_in.at[y_hi, x, core],
         load_sem.at[4],
     )
@@ -231,7 +236,8 @@
         if stage:
             source = query_in.at[slots[stage]]
         else:
-            source = queries.at[:, pl.ds(pl.multiple_of(partner * SLICE, 128), SLICE)]
+            begin = pl.multiple_of(slice_of(z, 1 - b) * SLICE, 128)
+            source = queries.at[:, pl.ds(begin, SLICE)]
         copy = query_copy(source, slots[stage], stage, peers[stage])
         copy.start()
         sent.append(copy)
@@ -352,25 +358,22 @@
         finish(first, count)
 
     turned[...] = jnp.concatenate([total[...], total[...]], axis=1)
-    lane = lax.broadcasted_iota(jnp.int32, (6, 2 * RANK), 1)
-    for t in range(N):
-        even = turned[pl.ds(12 * t, 6, stride=2), :]
-        odd = turned[pl.ds(12 * t + 1, 6, stride=2), :]
-        parts[t, :6, :] = jnp.where(lane < RANK, even, odd)
-
-    def other(r):
-        far, over = OTHERS[r]
-        return (z + far) % 8 * 2 + (1 - b if over else b)
-
-    def exchange(source, target, sends, recvs):
+    lane = lax.broadcasted_iota(jnp.int32, (LINES, 2 * RANK), 1)
+    for i in range(SLICES):
+        even = turned[pl.ds(2 * LINES * i, LINES, stride=2), :]
+        odd = turned[pl.ds(2 * LINES * i + 1, LINES, stride=2), :]
+        parts[i, :LINES, :] = jnp.where(lane < RANK, even, odd)
+
+    def exchange(ways, peer_of, source, target, sends, recvs):
         copies = []
-        for r in range(N - 1):
+        for r, (far, over) in enumerate(ways):
+            peer = (peer_of(far), 1 - b if over else b)
             copy = pltpu.make_async_remote_copy(
-                src_ref=source(other(r)),
-                dst_ref=target(r),
+                src_ref=source(*peer),
+                dst_ref=target,
                 send_sem=sends.at[r],
                 recv_sem=recvs.at[r],
-                device_id=(dp, other(r)),
+                device_id=(dp, peer[0] * 2 + peer[1]),
                 device_id_type=MESH,
             )
             copy.start()
@@ -378,15 +381,20 @@
         return copies
 
     to_sum = exchange(
-        lambda t: parts.at[t], lambda r: parts_in.at[r], parts_send, parts_recv
-    )
-    parts_in[N - 1] = parts[me]
+        OTHERS,
+        lambda far: (z + far) % 8,
+        lambda z, b: parts.at[slice_of(z, b)],
+        parts_in.at[me],
+        parts_send,
+        parts_recv,
+    )
+    parts_in[me] = parts[my_slice]
     for copy in to_sum:
         copy.wait_recv()
 
     entries = jnp.sum(parts_in[...], axis=0)
     squares = jnp.sum(entries * entries)
-    flat = jnp.concatenate([entries[i : i + 1, :] for i in range(6)], axis=1)
+    flat = jnp.concatenate([entries[i : i + 1, :] for i in range(LINES)], axis=1)
     high = flat.astype(jnp.bfloat16).astype(jnp.float32)
     row = lax.broadcasted_iota(jnp.int32, (16, SLICE), 0)
     pair = jnp.where(row == 0, high, jnp.where(row == 1, flat - high, 0.0))
@@ -398,9 +406,14 @@
     )
 
     to_add = exchange(
-        lambda t: tile, lambda r: tiles_in.at[me], tile_send, tile_recv
-    )
-    tiles_in[me] = tile[...]
+        NEAREST,
+        lambda far: (z + 8 - far) % 8,
+        lambda z, b: tile,
+        tiles_in.at[my_slice],
+        tile_send,
+        tile_recv,
+    )
+    tiles_in[my_slice] = tile[...]
     for copy in sent + to_sum:
         copy.wait_send()
     for copy in to_add:
@@ -437,11 +450,11 @@
             pltpu.VMEM((3 * RANK, 4 * ROWS), f32),
             pltpu.VMEM((3 * RANK, RANK), f32),
             pltpu.VMEM((3 * RANK, 2 * RANK), f32),
-            pltpu.VMEM((N, 8, 128), f32),
-            pltpu.VMEM((N, 8, 128), f32),
+            pltpu.VMEM((SLICES, 16, 128), f32),
+            pltpu.VMEM((N, 16, 128), f32),
             pltpu.VMEM((2, 4, 2, 16, SLICE), bf16),
             pltpu.VMEM((8, 128), f32),
-            pltpu.VMEM((N, 8, 128), f32),
+            pltpu.VMEM((SLICES, 8, 128), f32),
             pltpu.SMEM((1,), jnp.int32),
             dma((8 + PIECES,)),
             dma((N,)),

time: 53.8 us -> 52.7 us (0.980)
  Pallas kernels: 52.5 us -> 51.4 us
    pallas_call x1, Pallas kernels: 52.5 us -> 51.4 us  [per_device(): pl.pallas_call(kernel, out_shape=jax.ShapeDtypeStruct((1, N * 16), f32),...]
where the time goes in v4:
time: 52.7 us; the launch traced here: 52.6 us
  Pallas kernels  51.4 us (98%)
  between operations  0.66 us (1%)
  local copies, waits for them, and re-layouts  0.56 us (1%)
    pallas_call x1, Pallas kernels, per_device(): pl.pallas_call(kernel, out_shape=jax.ShapeDtypeStruct((1, N * 16), f32),...  51.4 us

profile of v4, /device:TPU:2, one launch (start us, length us, event | category | flops | bytes accessed | tf_op | source)
XLA Modules:
  0.0 52.6 jit_solution(9143957750415029012)
XLA Ops:
  0.7 51.4 %shard_map.82 = f32[1,256]{1,0:T(1,128)S(1)} custom-call(s32[1]{0:T(128)S(6)} %copy.10.lengths, bf16[32,4096]{1,0:T(8,128)(2,1)} %inputs.1, bf16[32,4096]{1,0:T(8,128)(2,1)} %cotangent.1, bf16[2,512,896]{2,1,0:T(8,128)(2,1)} %gate_up.1, bf16[896,4096]{1,0:T(8,128)(2,1)} %down_weight.1, bf16[192,4096]{1,0:T(8,128)(2,1)} %bitcast.2, bf16[192,896]{1,0:T(8,128)(2,1)} %bitcast.3, ...), custom_call_target="tpu_custom_call" | custom-call | flops 4000000000 | bytes 12000000 | tf_op jit(solution)/shard_map/pallas_call | solution.py:434
  52.1 0.6 %copy.11 = f32[1,256]{1,0:T(1,128)} copy(f32[1,256]{1,0:T(1,128)S(1)} %shard_map.82) | data formatting | bytes 2048

commit v5 on v4

--- a/solution.py
+++ b/solution.py
@@ -326,7 +326,7 @@
     for step in range(1, STEPS + 1):
         first, count = (0, 4) if step == 1 else (slot_of(step, 0), 3)
         for piece in range(PIECES):
-            for link in (DOWN, UP, ACROSS):
+            for link in (ACROSS, UP, DOWN):
                 pass_on(step, link, piece).wait_recv()
                 for later, way, slot in onward.get((step, link), ()):
                     send(later, way, piece, slot)

time: 52.7 us -> 52.8 us (level)
  no operation moved by 1% of the time
where the time goes in v5:
time: 52.8 us; the launch traced here: 52.7 us
  Pallas kernels  51.4 us (97%)
  between operations  0.66 us (1%)
  local copies, waits for them, and re-layouts  0.56 us (1%)
    pallas_call x1, Pallas kernels, per_device(): pl.pallas_call(kernel, out_shape=jax.ShapeDtypeStruct((1, N * 16), f32),...  51.4 us

profile of v5, /device:TPU:2, one launch (start us, length us, event | category | flops | bytes accessed | tf_op | source)
XLA Modules:
  0.0 52.7 jit_solution(16098243797012713301)
XLA Ops:
  0.7 51.4 %shard_map.82 = f32[1,256]{1,0:T(1,128)S(1)} custom-call(s32[1]{0:T(128)S(6)} %copy.10.lengths, bf16[32,4096]{1,0:T(8,128)(2,1)} %inputs.1, bf16[32,4096]{1,0:T(8,128)(2,1)} %cotangent.1, bf16[2,512,896]{2,1,0:T(8,128)(2,1)} %gate_up.1, bf16[896,4096]{1,0:T(8,128)(2,1)} %down_weight.1, bf16[192,4096]{1,0:T(8,128)(2,1)} %bitcast.2, bf16[192,896]{1,0:T(8,128)(2,1)} %bitcast.3, ...), custom_call_target="tpu_custom_call" | custom-call | flops 4000000000 | bytes 12000000 | tf_op jit(solution)/shard_map/pallas_call | solution.py:434
  52.1 0.6 %copy.11 = f32[1,256]{1,0:T(1,128)} copy(f32[1,256]{1,0:T(1,128)S(1)} %shard_map.82) | data formatting | bytes 2048

commit v6 on v5

--- a/solution.py
+++ b/solution.py
@@ -357,7 +357,7 @@
             wait_queries(4)
         finish(first, count)
 
-    turned[...] = jnp.concatenate([total[...], total[...]], axis=1)
+    turned[: 3 * RANK, :] = jnp.concatenate([total[...], total[...]], axis=1)
     lane = lax.broadcasted_iota(jnp.int32, (LINES, 2 * RANK), 1)
     for i in range(SLICES):
         even = turned[pl.ds(2 * LINES * i, LINES, stride=2), :]
@@ -449,7 +449,7 @@
             pltpu.VMEM((4 * ROWS, FF + RANK), f32),
             pltpu.VMEM((3 * RANK, 4 * ROWS), f32),
             pltpu.VMEM((3 * RANK, RANK), f32),
-            pltpu.VMEM((3 * RANK, 2 * RANK), f32),
+            pltpu.VMEM((3 * RANK + 8, 2 * RANK), f32),
             pltpu.VMEM((SLICES, 16, 128), f32),
             pltpu.VMEM((N, 16, 128), f32),
             pltpu.VMEM((2, 4, 2, 16, SLICE), bf16),

time: 52.8 us -> 52.8 us (level)
  no operation moved by 1% of the time
where the time goes in v6:
time: 52.8 us; the launch traced here: 52.7 us
  Pallas kernels  51.4 us (97%)
  between operations  0.66 us (1%)
  local copies, waits for them, and re-layouts  0.56 us (1%)
    pallas_call x1, Pallas kernels, per_device(): pl.pallas_call(kernel, out_shape=jax.ShapeDtypeStruct((1, N * 16), f32),...  51.4 us

profile of v6, /device:TPU:2, one launch (start us, length us, event | category | flops | bytes accessed | tf_op | source)
XLA Modules:
  0.0 52.7 jit_solution(580425218532108642)
XLA Ops:
  0.7 51.4 %shard_map.82 = f32[1,256]{1,0:T(1,128)S(1)} custom-call(s32[1]{0:T(128)S(6)} %copy.10.lengths, bf16[32,4096]{1,0:T(8,128)(2,1)} %inputs.1, bf16[32,4096]{1,0:T(8,128)(2,1)} %cotangent.1, bf16[2,512,896]{2,1,0:T(8,128)(2,1)} %gate_up.1, bf16[896,4096]{1,0:T(8,128)(2,1)} %down_weight.1, bf16[192,4096]{1,0:T(8,128)(2,1)} %bitcast.2, bf16[192,896]{1,0:T(8,128)(2,1)} %bitcast.3, ...), custom_call_target="tpu_custom_call" | custom-call | flops 4000000000 | bytes 12000000 | tf_op jit(solution)/shard_map/pallas_call | solution.py:434
  52.1 0.6 %copy.11 = f32[1,256]{1,0:T(1,128)} copy(f32[1,256]{1,0:T(1,128)S(1)} %shard_map.82) | data formatting | bytes 2048

commit v7 on v6

--- a/solution.py
+++ b/solution.py
@@ -184,13 +184,8 @@
     ]
     sent += first_sends
 
-    def send_first(turn):
-        @pl.when(core == turn)
-        def _():
-            for copy in first_sends:
-                copy.start()
-
-    send_first(0)
+    for copy in first_sends:
+        copy.start()
     load_ph.start()
     load_lengths.start()
     for copy in load_gates:
@@ -200,7 +195,6 @@
         copy.start()
     load_query.start()
     load_x.wait()
-    send_first(1)
     load_pm.wait()
     lead = dot(x_rows[...], pm[...], NT)
     for copy in load_own:

time: 52.8 us -> 52.7 us (level)
  no operation moved by 1% of the time
where the time goes in v7:
time: 52.7 us; the launch traced here: 52.6 us
  Pallas kernels  51.4 us (98%)
  between operations  0.66 us (1%)
  local copies, waits for them, and re-layouts  0.56 us (1%)
    pallas_call x1, Pallas kernels, per_device(): pl.pallas_call(kernel, out_shape=jax.ShapeDtypeStruct((1, N * 16), f32),...  51.4 us

profile of v7, /device:TPU:2, one launch (start us, length us, event | category | flops | bytes accessed | tf_op | source)
XLA Modules:
  0.0 52.6 jit_solution(17025631511670400960)
XLA Ops:
  0.7 51.4 %shard_map.82 = f32[1,256]{1,0:T(1,128)S(1)} custom-call(s32[1]{0:T(128)S(6)} %copy.10.lengths, bf16[32,4096]{1,0:T(8,128)(2,1)} %inputs.1, bf16[32,4096]{1,0:T(8,128)(2,1)} %cotangent.1, bf16[2,512,896]{2,1,0:T(8,128)(2,1)} %gate_up.1, bf16[896,4096]{1,0:T(8,128)(2,1)} %down_weight.1, bf16[192,4096]{1,0:T(8,128)(2,1)} %bitcast.2, bf16[192,896]{1,0:T(8,128)(2,1)} %bitcast.3, ...), custom_call_target="tpu_custom_call" | custom-call | flops 4000000000 | bytes 12000000 | tf_op jit(solution)/shard_map/pallas_call | solution.py:428
  52.1 0.6 %copy.11 = f32[1,256]{1,0:T(1,128)} copy(f32[1,256]{1,0:T(1,128)S(1)} %shard_map.82) | data formatting | bytes 2048
